TPU v7x, 32 devices: a whole 2x2x4 slice. The times are simulated.
32 devices in a mesh: group: 2 (over y), region: 4 (over z), probe: 4 (over x, core).
Axes of the slice: x: 2, y: 2, z: 4, core: 2. Of those that a mesh axis runs over, the one named last changes fastest.
Arguments:
- object_slices: float32 [4, 2, 512, 256], P('group', None, 'region', 'probe'), parts along dimension 0, may hold values from -4 to 4
- probe: float32 [4, 128, 128], P('group'), parts along dimension 0, may hold values from -6 to 6
- intensity: float32 [4, 16, 256, 128], P('region', 'probe', 'group'), parts along dimension 2, may hold values from 0.5 to 4
- positions: int32 [4, 16, 4], P('region', 'probe', 'group'), parts along dimension 2, may hold values from 0 to 255, as said below
Outputs:
- gradient: float32 [4, 2, 512, 256], P('group', None, 'region', 'probe'), parts along dimension 0
There are 2 independent parts, one for each index of `group`. A program takes and returns all parts, laid end to end along the dimension named above; each array names one. Nothing has to cross between parts.
Inputs may be any that keep to these rules, and one draw needn't show every extreme that they name: `positions`: entry 0 is a row offset below 128 within the region's rows, entry 1 a column offset below 256.
All inputs are finite; a program needn't handle non-finite values.
Results may differ from a plain program's by a relative error of at most 0.00014.
Values sent between devices are 32-bit elements; how exact they have to be, the bound alone decides.
A program may use at most 64 MiB of HBM per device.

v0:
```python
import math

import jax
import jax.numpy as jnp
from jax import lax
from jax.sharding import PartitionSpec as P


def from_behind(block, axis, distance):
    devices = range(lax.axis_size(axis))
    route = [((i - distance) % len(devices), i) for i in devices]
    return lax.ppermute(block, axis, route)


def propagator(window):
    indices = lax.iota(jnp.int32, window)
    frequency = (
        jnp.where(indices < window // 2, indices, indices - window).astype(jnp.float32) / window
    )
    phases = -60.0 * (frequency[:, None] ** 2 + frequency[None, :] ** 2)
    return (jnp.cos(phases), jnp.sin(phases))


def dft_tables(window):
    indices = lax.iota(jnp.int32, window)
    product = indices[:, None] * indices[None, :] % window
    angles = product.astype(jnp.float32) * (2.0 * math.pi / window)
    norm_factor = 1.0 / math.sqrt(window)
    return (jnp.cos(angles) * norm_factor, -jnp.sin(angles) * norm_factor)


def left_mul(matrix, values):
    return jnp.einsum("ab,nbc->nac", matrix, values, precision=lax.Precision.HIGHEST)


def right_mul(values, matrix):
    return jnp.einsum("nab,bc->nac", values, matrix, precision=lax.Precision.HIGHEST)


def transform(real_part, imag_part, table_re, table_im):
    left_re = left_mul(table_re, real_part) - left_mul(table_im, imag_part)
    left_im = left_mul(table_re, imag_part) + left_mul(table_im, real_part)
    out_re = right_mul(left_re, table_re) - right_mul(left_im, table_im)
    out_im = right_mul(left_re, table_im) + right_mul(left_im, table_re)
    return (out_re, out_im)


def fresnel(real_part, imag_part, table_re, table_im, kernel_re, kernel_im):
    spec_re, spec_im = transform(real_part, imag_part, table_re, table_im)
    moved_re = kernel_re * spec_re - kernel_im * spec_im
    moved_im = kernel_re * spec_im + kernel_im * spec_re
    return transform(moved_re, moved_im, table_re, -table_im)


def body(object_slices, probe, intensity, positions):
    layers = object_slices.shape[0]
    band_rows = object_slices.shape[2]
    window = probe.shape[1]
    item_count = positions.shape[1]
    lower_band = from_behind(object_slices, "region", -1)
    extended = jnp.concatenate([object_slices, lower_band], axis=2)
    whole_band = lax.all_gather(extended, "probe", axis=3, tiled=True)
    columns = whole_band.shape[3]
    padded = jnp.concatenate([whole_band, whole_band[:, :, :, :window]], axis=3)
    row_offsets = positions[0, :, 0]
    col_offsets = positions[0, :, 1]
    anchor = jnp.zeros((), jnp.int32)

    def cut_patch(row_offset, col_offset):
        return lax.dynamic_slice(
            padded, (anchor, anchor, row_offset, col_offset), (layers, 2, window, window)
        )

    patches = jax.vmap(cut_patch)(row_offsets, col_offsets)
    table_re, table_im = dft_tables(window)
    kernel_re, kernel_im = propagator(window)
    wave_re = jnp.broadcast_to(probe[0], (item_count, window, window))
    wave_im = jnp.broadcast_to(probe[1], (item_count, window, window))
    incident = []
    exit_re = wave_re
    exit_im = wave_im
    for layer in range(layers):
        incident.append((wave_re, wave_im))
        patch_re = patches[:, layer, 0]
        patch_im = patches[:, layer, 1]
        exit_re = wave_re * patch_re - wave_im * patch_im
        exit_im = wave_re * patch_im + wave_im * patch_re
        if layer < layers - 1:
            wave_re, wave_im = fresnel(exit_re, exit_im, table_re, table_im, kernel_re, kernel_im)
    far_re, far_im = transform(exit_re, exit_im, table_re, table_im)
    misfit = far_re * far_re + far_im * far_im - intensity[0]
    back_re, back_im = transform(misfit * far_re, misfit * far_im, table_re, -table_im)
    layer_grads = [None] * layers
    for layer in reversed(range(layers)):
        wave_re, wave_im = incident[layer]
        layer_grads[layer] = jnp.stack(
            [wave_re * back_re + wave_im * back_im, wave_re * back_im - wave_im * back_re], axis=1
        )
        if layer > 0:
            patch_re = patches[:, layer, 0]
            patch_im = patches[:, layer, 1]
            carried_re = patch_re * back_re + patch_im * back_im
            carried_im = patch_re * back_im - patch_im * back_re
            back_re, back_im = fresnel(
                carried_re, carried_im, table_re, table_im, kernel_re, -kernel_im
            )
    gradients = jnp.stack(layer_grads, axis=1)

    def deposit(position, accumulated):
        corner = (anchor, anchor, row_offsets[position], col_offsets[position])
        current = lax.dynamic_slice(accumulated, corner, (layers, 2, window, window))
        return lax.dynamic_update_slice(accumulated, current + gradients[position], corner)

    accumulated = lax.fori_loop(0, item_count, deposit, jnp.zeros(padded.shape, jnp.float32))
    wrapped_head = accumulated[:, :, :, :window] + accumulated[:, :, :, columns:]
    folded = jnp.concatenate([wrapped_head, accumulated[:, :, :, window:columns]], axis=3)
    upper_part = folded[:, :, :band_rows]
    spill_rows = folded[:, :, band_rows:]
    returned = from_behind(spill_rows, "region", 1)
    summed = lax.psum_scatter(upper_part + returned, "probe", scatter_dimension=3, tiled=True)
    return summed * (1.0 / (item_count * lax.axis_size("probe")))


def solution(mesh):
    placed = (
        P("group", None, "region", "probe"),
        P("group", None, None),
        P("region", "probe", "group", None),
        P("region", "probe", "group"),
    )
    return jax.shard_map(
        body,
        mesh=mesh,
        in_specs=placed,
        out_specs=P("group", None, "region", "probe"),
        check_vma=False,
    )
```

profile of v0, /device:TPU:0, one launch (start us, length us, event | category | flops | bytes accessed | tf_op | source)
XLA Modules:
  0.0 167.1 jit_solution(12580402229340034271)
XLA Ops:
  6.5 1.0 copy.66
  7.5 5.1 %collective-permute-start = (f32[2,2,128,64]{2,1,0,3:T(2,128)S(1)}, f32[2,2,128,64]{2,1,0,3:T(2,128)S(1)}, u32[]{:S(2)}, u32[]{:S(2)}) collective-permute-start(f32[2,2,128,64]{2,1,0,3:T(2,128)S(1)} %copy.66), channel_id=1, source_target_pairs={{4,0},{8,4},{12,8},{0,12},{5,1},{9,5},{13,9},{1,13},{6,2},{10,6},{... | collective-permute-start | bytes 393224 | tf_op jit(solution)/shard_map/ppermute | solution.py:12
  12.6 2.8 %collective-permute-done = f32[2,2,128,64]{2,1,0,3:T(2,128)S(1)} collective-permute-done((f32[2,2,128,64]{2,1,0,3:T(2,128)S(1)}, f32[2,2,128,64]{2,1,0,3:T(2,128)S(1)}, u32[]{:S(2)}, u32[]{:S(2)}) %collective-permute-start) | collective-permute-done | bytes 131104 | tf_op jit(solution)/shard_map/ppermute | solution.py:12
  15.4 0.8 pad_maximum_fusion.3
  16.3 0.8 compare_select_fusion.1
  17.3 0.8 slice_bitcast_fusion.2
  18.1 0.9 slice_bitcast_fusion.1
  19.3 15.7 %all-gather.2.cloned.1.call-done = f32[2,2,256,256]{2,1,0,3:T(2,128)} async-done(((f32[2,2,256,64]{2,1,0,3:T(2,128)}), f32[2,2,256,256]{2,1,0,3:T(2,128)}) %all-gather.2.cloned.1.call-update) | async-done | bytes 1048592 | tf_op jit(solution)/shard_map/all_gather | solution.py:62
  35.1 1.3 slice.77
  37.1 10.2 %while.15 = (s32[]{:T(128)}, f32[2,2,256,384]{2,1,0,3:T(2,128)S(1)}, s32[4,4]{1,0:T(4,128)S(1)}, f32[4,2,2,128,128]{4,3,0,2,1:T(8,128)S(1)}, s32[]{:T(128)}) while((s32[]{:T(128)}, f32[2,2,256,384]{2,1,0,3:T(2,128)S(1)}, s32[4,4]{1,0:T(4,128)S(1)}, f32[4,2,2,128,128]{4,3,0,2,1:T(8,128)S(1)}, s32[]{:T(128)}) %tuple.59), condition=%wide.while_cond, body=%wide.while_body.sunk | while | flops 2 | bytes 1572997 | solution.py:70
  37.8 1.6 constant_dynamic-slice_fusion.8
  40.3 1.6 constant_dynamic-slice_fusion.8
  42.8 1.6 constant_dynamic-slice_fusion.8
  45.3 1.6 constant_dynamic-slice_fusion.8
  47.3 0.8 fusion.95
  48.1 0.8 fusion.11
  48.9 0.7 fusion.50
  50.3 0.8 fusion.91
  51.1 0.8 fusion.10
  52.6 0.7 convolution_subtract_fusion.10
  53.3 0.8 fusion.84
  54.1 0.8 fusion.88
  54.9 0.8 fusion.9
  57.1 0.8 fusion.8
  58.6 0.9 fusion.15
  64.7 0.7 convolution_subtract_fusion.6
  65.4 0.8 fusion.70
  66.2 0.8 fusion.74
  67.0 0.8 fusion.5
  69.2 0.8 fusion.4
  70.7 1.2 fusion.17
  77.0 0.7 convolution_subtract_fusion.2
  77.7 0.8 fusion.56
  78.5 0.8 fusion.60
  79.3 0.8 fusion.1
  81.5 0.8 fusion
  82.3 0.9 convolution_add_fusion
  83.2 0.7 add_bitcast_fusion.1
  84.3 35.3 %while.14 = (s32[]{:T(128)}, f32[2,2,256,384]{2,3,1,0:T(8,128)S(1)}, s32[4]{0:T(128)S(1)}, s32[4]{0:T(128)S(1)}, f32[4,2,2,128,128]{4,3,0,2,1:T(8,128)S(1)}, /*index=5*/s32[]{:T(128)}, s32[]{:T(128)}, s32[]{:T(128)}, s32[]{:T(128)}) while((s32[]{:T(128)}, f32[2,2,256,384]{2,3,1,0:T(8,128)S(1)}, s32[4]{0:T(128)S(1)}, s32[4]{0:T(128)S(1)}, ...), condition=%wide.region_1.2_spmd, body=%wide.region_0.1_spmd.sunk | while | flops 65544 | bytes 2883793 | solution.py:114
  90.2 3.0 %dynamic_update_slice.8 = f32[2,2,256,384]{2,3,1,0:T(8,128)S(1)} dynamic-update-slice(f32[2,2,256,384]{2,3,1,0:T(8,128)S(1)} %get-tuple-element.251, f32[2,2,128,128]{2,3,1,0:T(8,128)S(1)} %copy.185, s32[]{:T(128)} %constant.61.clone.1..sunk, s32[]{:T(128)} %constant.61.clone.1..sunk, s32[]{:T(128)S(6)} %select_n.346, s32[]{:T(128)S(6)} %select_n.347) | dynamic-update-slice | bytes 524292 | tf_op jit(solution)/shard_map/while/body/eval_jaxpr/dynamic_update_slice | solution.py:112
  99.3 1.8 %dynamic_update_slice.8 = f32[2,2,256,384]{2,3,1,0:T(8,128)S(1)} dynamic-update-slice(f32[2,2,256,384]{2,3,1,0:T(8,128)S(1)} %get-tuple-element.251, f32[2,2,128,128]{2,3,1,0:T(8,128)S(1)} %copy.185, s32[]{:T(128)} %constant.61.clone.1..sunk, s32[]{:T(128)} %constant.61.clone.1..sunk, s32[]{:T(128)S(6)} %select_n.346, s32[]{:T(128)S(6)} %select_n.347) | dynamic-update-slice | bytes 524292 | tf_op jit(solution)/shard_map/while/body/eval_jaxpr/dynamic_update_slice | solution.py:112
  107.1 3.3 %dynamic_update_slice.8 = f32[2,2,256,384]{2,3,1,0:T(8,128)S(1)} dynamic-update-slice(f32[2,2,256,384]{2,3,1,0:T(8,128)S(1)} %get-tuple-element.251, f32[2,2,128,128]{2,3,1,0:T(8,128)S(1)} %copy.185, s32[]{:T(128)} %constant.61.clone.1..sunk, s32[]{:T(128)} %constant.61.clone.1..sunk, s32[]{:T(128)S(6)} %select_n.346, s32[]{:T(128)S(6)} %select_n.347) | dynamic-update-slice | bytes 524292 | tf_op jit(solution)/shard_map/while/body/eval_jaxpr/dynamic_update_slice | solution.py:112
  116.3 3.2 %dynamic_update_slice.8 = f32[2,2,256,384]{2,3,1,0:T(8,128)S(1)} dynamic-update-slice(f32[2,2,256,384]{2,3,1,0:T(8,128)S(1)} %get-tuple-element.251, f32[2,2,128,128]{2,3,1,0:T(8,128)S(1)} %copy.185, s32[]{:T(128)} %constant.61.clone.1..sunk, s32[]{:T(128)} %constant.61.clone.1..sunk, s32[]{:T(128)S(6)} %select_n.346, s32[]{:T(128)S(6)} %select_n.347) | dynamic-update-slice | bytes 524292 | tf_op jit(solution)/shard_map/while/body/eval_jaxpr/dynamic_update_slice | solution.py:112
  119.7 3.4 %collective-permute-start.1 = (f32[2,2,128,256]{2,3,1,0:T(8,128)S(1)}, f32[2,2,128,256]{2,3,1,0:T(8,128)S(1)}, u32[]{:S(2)}, u32[]{:S(2)}) collective-permute-start(f32[2,2,128,256]{2,3,1,0:T(8,128)S(1)} %pad_maximum_fusion.2), channel_id=1, source_target_pairs={{12,0},{0,4},{4,8},{8,12},{13,1},{1,5},{5,9},{9,13},{14,2},{2,6},{... | collective-permute-start | bytes 1572872 | tf_op jit(solution)/shard_map/ppermute | solution.py:12
  123.0 13.3 %collective-permute-done.1 = f32[2,2,128,256]{2,3,1,0:T(8,128)S(1)} collective-permute-done((f32[2,2,128,256]{2,3,1,0:T(8,128)S(1)}, f32[2,2,128,256]{2,3,1,0:T(8,128)S(1)}, u32[]{:S(2)}, u32[]{:S(2)}) %collective-permute-start.1) | collective-permute-done | bytes 524320 | tf_op jit(solution)/shard_map/ppermute | solution.py:12
  136.4 0.9 fusion.13
  137.3 21.2 %reduce-scatter.2.cloned.1.call-done = f32[2,2,128,64]{2,3,1,0:T(8,128)} async-done(((f32[2,2,128,256]{2,3,1,0:T(8,128)}), f32[2,2,128,64]{2,3,1,0:T(8,128)}) %reduce-scatter.2.cloned.1.call-update) | async-done | bytes 131088 | tf_op jit(solution)/shard_map/reduce_scatter | solution.py:120
  158.5 1.6 broadcast_multiply_fusion
  (86 shorter events, 29.7 us)
Async XLA Ops:
  6.5 28.5 %all-gather.2.cloned.1.call-start = ((), (), s32[]{:S(2)}) async-start(), calls=%async_computation.1 | async-start | bytes 1310720 | tf_op jit(solution)/shard_map/all_gather | solution.py:62
  7.5 7.9 %collective-permute-start = (f32[2,2,128,64]{2,1,0,3:T(2,128)S(1)}, f32[2,2,128,64]{2,1,0,3:T(2,128)S(1)}, u32[]{:S(2)}, u32[]{:S(2)}) collective-permute-start(f32[2,2,128,64]{2,1,0,3:T(2,128)S(1)} %copy.66), channel_id=1, source_target_pairs={{4,0},{8,4},{12,8},{0,12},{5,1},{9,5},{13,9},{1,13},{6,2},{10,6},{... | collective-permute-start | bytes 393224 | tf_op jit(solution)/shard_map/ppermute | solution.py:12
  16.3 142.2 %reduce-scatter.2.cloned.1.call-start = ((), (), s32[]{:S(2)}) async-start(), calls=%async_computation.2 | async-start | bytes 655360 | tf_op jit(solution)/shard_map/reduce_scatter | solution.py:120
  35.1 1.4 copy-start.1
  62.5 2.9 %copy-start = (f32[1,4,128,128]{3,2,1,0:T(8,128)S(1)}, f32[1,4,128,128]{3,2,1,0:T(8,128)}, u32[]{:S(2)}) copy-start(f32[1,4,128,128]{3,2,1,0:T(8,128)} %param.8) | copy-start | bytes 786436
  119.7 16.7 %collective-permute-start.1 = (f32[2,2,128,256]{2,3,1,0:T(8,128)S(1)}, f32[2,2,128,256]{2,3,1,0:T(8,128)S(1)}, u32[]{:S(2)}, u32[]{:S(2)}) collective-permute-start(f32[2,2,128,256]{2,3,1,0:T(8,128)S(1)} %pad_maximum_fusion.2), channel_id=1, source_target_pairs={{12,0},{0,4},{4,8},{8,12},{13,1},{1,5},{5,9},{9,13},{14,2},{2,6},{... | collective-permute-start | bytes 1572872 | tf_op jit(solution)/shard_map/ppermute | solution.py:12
Sparse Core Ops, SparseCore 0:
  16.4 18.6 all-gather.1
  137.4 21.0 reduce-scatter.1
where the time goes:
time: 170 us; the launch traced here: 167 us
  waiting for transfers between devices  53.1 us (31%)
  matrix products  36.3 us (21%)
  local copies, waits for them, and re-layouts  32.5 us (19%)
  loops' own time  17.2 us (10%)
  between operations  14 us (8%)
  starting transfers between devices  8.5 us (5%)
  other arithmetic  5.53 us (3%)
    reduce_scatter x1, waiting for transfers between devices, body(): lax.psum_scatter(upper_part + returned, 'probe', scatter_dimension=3, til...  21.2 us
    dot_general x24, matrix products, right_mul(): jnp.einsum('nab,bc->nac', values, matrix, precision=lax.Precision.HIGHEST)  18.2 us
    dot_general x24, matrix products, left_mul(): jnp.einsum('ab,nbc->nac', matrix, values, precision=lax.Precision.HIGHEST)  18.1 us
    another operation x1, loops' own time, body(): lax.fori_loop(0, item_count, deposit, jnp.zeros(padded.shape, jnp.float32))  16.8 us
    ppermute x2, waiting for transfers between devices, from_behind(): return lax.ppermute(block, axis, route)  16.1 us
    all_gather x1, waiting for transfers between devices, body(): whole_band = lax.all_gather(extended, 'probe', axis=3, tiled=True)  15.7 us
    dynamic_update_slice x8, local copies, waits for them, and re-layouts, deposit(): lax.dynamic_update_slice(accumulated, current + gradients[position], corner)  11.9 us
    gather x20, local copies, waits for them, and re-layouts  9.85 us
  transfers between devices with their start and end apart: 4, of which 4 were waited for; matrix products, arithmetic and copies ran while one was open for 2% of the time, Pallas kernels for 0%

commit v1 on v0

v1 whole, which is shorter than its diff:
```python
import functools
import math

import jax
import jax.numpy as jnp
import ml_dtypes
import numpy as np
from jax import lax
from jax.experimental import pallas as pl
from jax.experimental.pallas import tpu as pltpu
from jax.sharding import PartitionSpec as P

MESH = pl.DeviceIdType.MESH
VMEM_BYTES = 48 * 1024 * 1024


def halves(matrix):
    high = matrix.astype(np.float32).astype(ml_dtypes.bfloat16)
    low = (matrix - high.astype(np.float64)).astype(np.float32).astype(ml_dtypes.bfloat16)
    return high, low


def tables(window):
    index = np.arange(window)
    angle = (index[:, None] * index[None, :] % window) * (2.0 * math.pi / window)
    re = np.cos(angle) / math.sqrt(window)
    im = -np.sin(angle) / math.sqrt(window)
    forward = np.block([[re, im], [-im, re]])
    high, low = halves(forward)
    high_t, low_t = halves(forward.T)
    frequency = np.where(index < window // 2, index, index - window) / window
    phase = -60.0 * (frequency[:, None] ** 2 + frequency[None, :] ** 2)
    mover = np.stack([np.cos(phase), np.sin(phase)]).astype(np.float32)
    return np.stack([high, low, high_t, low_t]), mover


def split(values):
    high = values.astype(jnp.bfloat16)
    low = (values - high.astype(jnp.float32)).astype(jnp.bfloat16)
    return high, low


def product(left, right):
    dot = functools.partial(jnp.dot, preferred_element_type=jnp.float32)
    return dot(left[0], right[0]) + (dot(left[1], right[0]) + dot(left[0], right[1]))


def kernel(
    sizes, pos_ref, obj_ref, probe_ref, intensity_ref, table_ref, mover_ref, out_ref,
    tiles, canvas, spread, give, take, total, final,
    tile_send, tile_recv, sum_send, sum_recv,
):
    layers, chips, regions, items, window = sizes
    columns = chips * window
    half = window // 2
    me = lax.axis_index("probe")
    band = lax.axis_index("region")
    chip = me // 2
    core = me % 2
    twin = {"probe": me + 1 - 2 * core, "region": band}
    places = [(b, d) for b in range(2) for d in range(chips)]
    first = core == 0
    lane = lax.broadcasted_iota(jnp.int32, (window, window), 1)
    in_left = lane < half

    def device(shift, band_shift):
        return {
            "probe": (chip + chips + shift) % chips * 2 + core,
            "region": (band + regions + band_shift) % regions,
        }

    barrier = pltpu.get_barrier_semaphore()
    peers = [twin] + [
        device(d, b) for d in range(chips) for b in (0, -1, 1) if (d, b) != (0, 0)
    ]
    for peer in peers:
        pl.semaphore_signal(barrier, inc=1, device_id=peer, device_id_type=MESH)
    for layer in range(layers):
        tiles[layer, 0, 0, 0] = jnp.concatenate([obj_ref[layer, 0], obj_ref[layer, 1]], axis=1)
    margin = jnp.zeros((window, window), jnp.float32)
    for n in range(items):
        for plane in range(2):
            for d in range(chips):
                spread[n, plane, d, 0:window] = margin
                spread[n, plane, d, 2 * window : 3 * window] = margin
    pl.semaphore_wait(barrier, len(peers))

    def tile_copy(layer, b, d):
        return pltpu.make_async_remote_copy(
            src_ref=tiles.at[layer, 0, 0, 0],
            dst_ref=tiles.at[layer, b, d, 0],
            send_sem=tile_send.at[layer, b, d, 0],
            recv_sem=tile_recv.at[layer, b, d, 0],
            device_id=device(-d, -b),
            device_id_type=MESH,
        )

    def tile_pass(layer, b, d):
        return pltpu.make_async_remote_copy(
            src_ref=tiles.at[layer, b, d, 0],
            dst_ref=tiles.at[layer, b, d, 1],
            send_sem=tile_send.at[layer, b, d, 1],
            recv_sem=tile_recv.at[layer, b, d, 1],
            device_id=twin,
            device_id_type=MESH,
        )

    def sum_pass(layer, b, d):
        return pltpu.make_async_remote_copy(
            src_ref=give.at[layer, b, d],
            dst_ref=take.at[layer, b, d],
            send_sem=sum_send.at[layer, b, d, 0],
            recv_sem=sum_recv.at[layer, b, d, 0],
            device_id=twin,
            device_id_type=MESH,
        )

    def sum_copy(layer, b, d):
        return pltpu.make_async_remote_copy(
            src_ref=total.at[layer, b, d],
            dst_ref=final.at[layer, b, d],
            send_sem=sum_send.at[layer, b, d, 1],
            recv_sem=sum_recv.at[layer, b, d, 1],
            device_id=device(d, b),
            device_id_type=MESH,
        )

    away = places[1:]
    for layer in range(layers):
        for b, d in away:
            tile_copy(layer, b, d).start()
        tile_pass(layer, 0, 0).start()

    def relay(layer):
        for b, d in away:
            tile_copy(layer, b, d).wait_recv()
            tile_pass(layer, b, d).start()

    def assemble(layer):
        for b, d in places:
            tile_pass(layer, b, d).wait_recv()
            same, other = tiles[layer, b, d, 0], tiles[layer, b, d, 1]
            west = jnp.where(first, same, other)
            east = jnp.where(first, other, same)
            rows = slice(b * window, (b + 1) * window)
            canvas[layer, 0, d, rows] = jnp.where(in_left, west, pltpu.roll(east, half, 1))
            canvas[layer, 1, d, rows] = jnp.where(in_left, pltpu.roll(west, half, 1), east)

    row = [pos_ref[0, n, 0] for n in range(items)]
    col = [(pos_ref[0, n, 1] + columns - chip * window) % columns for n in range(items)]

    def cut(layer):
        patches = []
        for n in range(items):
            both = []
            for plane in range(2):
                strip = jnp.concatenate(
                    [canvas[layer, plane, d, pl.ds(row[n], window), :] for d in range(chips)],
                    axis=1,
                )
                both.append(pltpu.roll(strip, (columns - col[n]) % columns, 1)[:, :window])
            patches.append(tuple(both))
        return patches

    def on_rows(waves, which):
        stacked = jnp.concatenate([jnp.concatenate(w, axis=1) for w in waves], axis=0)
        matrix = (table_ref[2 * which], table_ref[2 * which + 1])
        out = product(split(stacked), matrix)
        return [
            (out[n * window : (n + 1) * window, :window], out[n * window : (n + 1) * window, window:])
            for n in range(len(waves))
        ]

    def on_columns(waves, which):
        stacked = jnp.concatenate([jnp.concatenate(w, axis=0) for w in waves], axis=1)
        matrix = (table_ref[2 - 2 * which], table_ref[3 - 2 * which])
        out = product(matrix, split(stacked))
        return [
            (out[:window, n * window : (n + 1) * window], out[window:, n * window : (n + 1) * window])
            for n in range(len(waves))
        ]

    def forward(waves):
        return on_rows(on_columns(waves, 0), 0)

    def backward(waves):
        return on_columns(on_rows(waves, 1), 1)

    def times(a, b):
        return (a[0] * b[0] - a[1] * b[1], a[0] * b[1] + a[1] * b[0])

    def conj_times(a, b):
        return (a[0] * b[0] + a[1] * b[1], a[0] * b[1] - a[1] * b[0])

    mover = (mover_ref[0], mover_ref[1])

    def scatter(layer, grads):
        blank = jnp.zeros((window, columns - window), jnp.float32)
        for n in range(items):
            for plane in range(2):
                wide = jnp.concatenate([grads[n][plane], blank], axis=1)
                wide = pltpu.roll(wide, col[n], 1)
                for d in range(chips):
                    spread[n, plane, d, window : 2 * window] = wide[:, d * window : (d + 1) * window]
        for b, d in places:
            re, im = [
                sum(
                    spread[n, plane, d, pl.ds((b + 1) * window - row[n], window), :]
                    for n in range(items)
                )
                for plane in range(2)
            ]
            west = jnp.where(in_left, re, pltpu.roll(im, half, 1))
            east = jnp.where(in_left, pltpu.roll(re, half, 1), im)
            total[layer, b, d] = jnp.where(first, west, east)
            give[layer, b, d] = jnp.where(first, east, west)
            sum_pass(layer, b, d).start()

    def share(layer):
        for b, d in away + places[:1]:
            sum_pass(layer, b, d).wait_recv()
            total[layer, b, d] = total[layer, b, d] + take[layer, b, d]
            if (b, d) != (0, 0):
                sum_copy(layer, b, d).start()

    relay(0)
    assemble(0)
    incident = [[(probe_ref[0], probe_ref[1])] * items]
    patches = []
    for layer in range(layers):
        patches.append(cut(layer))
        leaving = [times(w, p) for w, p in zip(incident[layer], patches[layer])]
        far = forward(leaving)
        if layer < layers - 1:
            relay(layer + 1)
            incident.append(backward([times(mover, w) for w in far]))
            assemble(layer + 1)
    residual = []
    for n in range(items):
        re, im = far[n]
        misfit = re * re + im * im - intensity_ref[0, n]
        residual.append((misfit * re, misfit * im))
    back = backward(residual)
    for layer in reversed(range(layers)):
        scatter(layer, [conj_times(w, g) for w, g in zip(incident[layer], back)])
        if layer > 0:
            far = forward([conj_times(p, g) for p, g in zip(patches[layer], back)])
            share(layer)
            back = backward([conj_times(mover, w) for w in far])
    share(0)
    scale = 1.0 / (items * 2 * chips)
    for layer in reversed(range(layers)):
        value = total[layer, 0, 0]
        for b, d in away:
            sum_copy(layer, b, d).wait_recv()
            value = value + final[layer, b, d]
        value = value * scale
        out_ref[layer, 0] = value[:, :half]
        out_ref[layer, 1] = value[:, half:]
    for layer in range(layers):
        for b, d in places:
            tile_pass(layer, b, d).wait_send()
            sum_pass(layer, b, d).wait_send()
        for b, d in away:
            tile_copy(layer, b, d).wait_send()
            sum_copy(layer, b, d).wait_send()


def body(object_slices, probe, intensity, positions):
    layers = object_slices.shape[0]
    window = probe.shape[1]
    items = positions.shape[1]
    chips = lax.axis_size("probe") // 2
    regions = lax.axis_size("region")
    table, mover = tables(window)
    f32 = jnp.float32
    whole = pl.BlockSpec(memory_space=pltpu.VMEM)
    return pl.pallas_call(
        functools.partial(kernel, (layers, chips, regions, items, window)),
        out_shape=jax.ShapeDtypeStruct(object_slices.shape, f32),
        in_specs=[pl.BlockSpec(memory_space=pltpu.SMEM)] + [whole] * 5,
        out_specs=whole,
        scratch_shapes=[
            pltpu.VMEM((layers, 2, chips, 2, window, window), f32),
            pltpu.VMEM((layers, 2, chips, 2 * window, window), f32),
            pltpu.VMEM((items, 2, chips, 3 * window, window), f32),
            pltpu.VMEM((layers, 2, chips, window, window), f32),
            pltpu.VMEM((layers, 2, chips, window, window), f32),
            pltpu.VMEM((layers, 2, chips, window, window), f32),
            pltpu.VMEM((layers, 2, chips, window, window), f32),
        ]
        + [pltpu.SemaphoreType.DMA((layers, 2, chips, 2))] * 4,
        compiler_params=pltpu.CompilerParams(
            collective_id=0, has_side_effects=True, vmem_limit_bytes=VMEM_BYTES
        ),
    )(positions, object_slices, probe, intensity, jnp.asarray(table), jnp.asarray(mover))


def solution(mesh):
    placed = (
        P("group", None, "region", "probe"),
        P("group", None, None),
        P("region", "probe", "group", None),
        P("region", "probe", "group"),
    )
    return jax.shard_map(
        body,
        mesh=mesh,
        in_specs=placed,
        out_specs=P("group", None, "region", "probe"),
        check_vma=False,
    )
```

time: 170 us -> 34.9 us (0.21); the launches traced: 167 us -> 34.7 us
  waiting for transfers between devices: 53.1 us -> 0 us
  matrix products: 36.3 us -> 0 us
  Pallas kernels: 0 us -> 30.1 us
  local copies, waits for them, and re-layouts: 32.5 us -> 4.6 us
  loops' own time: 17.2 us -> 0 us
  between operations: 14 us -> 0.04 us
  starting transfers between devices: 8.5 us -> 0 us
  other arithmetic: 5.53 us -> 0 us
    dot_general x48 -> x0, matrix products: 36.3 us -> none  [the longest x24 18.2 us: right_mul(): jnp.einsum('nab,bc->nac', values, matrix, precision=lax.Precision.HIGHEST)]
    pallas_call x0 -> x1, Pallas kernels: none -> 30.1 us  [body(): pl.pallas_call(functools.partial(kernel, (layers, chips, regions, items,...]
    reduce_scatter x1 -> x0, waiting for transfers between devices: 21.2 us -> none  [body(): lax.psum_scatter(upper_part + returned, 'probe', scatter_dimension=3, til...]
    another operation x2 -> x0, loops' own time: 17.2 us -> none  [the longest x1 16.8 us: body(): lax.fori_loop(0, item_count, deposit, jnp.zeros(padded.shape, jnp.float32))]
    ppermute x2 -> x0, waiting for transfers between devices: 16.1 us -> none  [from_behind(): return lax.ppermute(block, axis, route)]
    all_gather x1 -> x0, waiting for transfers between devices: 15.7 us -> none  [body(): whole_band = lax.all_gather(extended, 'probe', axis=3, tiled=True)]
    dynamic_update_slice x8 -> x0, local copies, waits for them, and re-layouts: 11.9 us -> none  [deposit(): lax.dynamic_update_slice(accumulated, current + gradients[position], corner)]
    gather x20 -> x0, local copies, waits for them, and re-layouts: 9.85 us -> none
  transfers between devices with their start and end apart: 4 -> 0, of which waited for: 4 -> 0; matrix products, arithmetic and copies ran while one was open for 2% -> 0% of each run, Pallas kernels for 0% -> 0%
where the time goes in v1:
time: 34.9 us; the launch traced here: 34.7 us
  Pallas kernels  30.1 us (86%)
  local copies, waits for them, and re-layouts  4.6 us (13%)
    pallas_call x1, Pallas kernels, body(): pl.pallas_call(functools.partial(kernel, (layers, chips, regions, items,...  30.1 us
    unnamed x10, local copies, waits for them, and re-layouts  3.82 us
    pallas_call x1, local copies, waits for them, and re-layouts, body(): pl.pallas_call(functools.partial(kernel, (layers, chips, regions, items,...  0.77 us

profile of v1, /device:TPU:0, one launch (start us, length us, event | category | flops | bytes accessed | tf_op | source)
XLA Modules:
  0.0 34.7 jit_solution(15790404021073376255)
XLA Ops:
  0.0 0.0 copy-start.1
  0.0 0.8 %copy.7.pos_ref = s32[1,4,2]{2,1,0:T(4,128)S(1)} copy(s32[1,4,2]{1,2,0:T(2,128)} %param.9) | data formatting | bytes 64 | tf_op args[3]
  0.8 0.0 copy-start.2
  0.8 1.1 %copy.8.obj_ref = f32[2,2,128,64]{3,2,1,0:T(8,128)S(1)} copy(f32[2,2,128,64]{2,3,1,0:T(8,128)} %param.6) | data formatting | bytes 262144 | tf_op args[0]
  1.9 0.0 copy-done.1
  1.9 0.0 copy-done.2
  1.9 0.0 copy-start
  1.9 1.0 %copy-done = bf16[4,256,256]{2,1,0:T(8,128)(2,1)S(1)} copy-done((bf16[4,256,256]{2,1,0:T(8,128)(2,1)S(1)}, bf16[4,256,256]{2,1,0:T(8,128)(2,1)}, u32[]{:S(2)}) %copy-start) | copy-done | bytes 524312
  3.0 0.0 copy-start.3
  3.0 0.9 %copy-done.3 = f32[2,128,128]{2,1,0:T(8,128)S(1)} copy-done((f32[2,128,128]{2,1,0:T(8,128)S(1)}, f32[2,128,128]{2,1,0:T(8,128)}, u32[]{:S(2)}) %copy-start.3) | copy-done | bytes 131096
  3.9 30.1 %shard_map.64 = f32[2,2,128,64]{3,2,1,0:T(8,128)S(1)} custom-call(s32[1,4,2]{2,1,0:T(4,128)S(1)} %copy.7.pos_ref, f32[2,2,128,64]{3,2,1,0:T(8,128)S(1)} %copy.8.obj_ref, f32[2,128,128]{2,1,0:T(8,128)S(1)} %copy-done.2, f32[1,4,128,128]{3,2,1,0:T(8,128)S(1)} %copy-done.1, bf16[4,256,256]{2,1,0:T(8,128)(2,1)S(1)} %copy-done, f32[2,128,128]{2,1,0:T(8,128)S(1)} %copy-done.3), custom_call_target="tpu_custom_call" | custom-call | tf_op jit(solution)/shard_map/pallas_call | solution.py:278
  33.9 0.8 %copy.9 = f32[2,2,128,64]{2,3,1,0:T(8,128)} copy(f32[2,2,128,64]{3,2,1,0:T(8,128)S(1)} %shard_map.64) | data formatting | bytes 262144 | tf_op jit(solution)/shard_map/pallas_call | solution.py:278
Async XLA Ops:
  0.0 1.9 %copy-start.1 = (f32[1,4,128,128]{3,2,1,0:T(8,128)S(1)}, f32[1,4,128,128]{3,2,1,0:T(8,128)}, u32[]{:S(2)}) copy-start(f32[1,4,128,128]{3,2,1,0:T(8,128)} %intensity_ref.1) | copy-start | bytes 786436
  0.8 1.1 %copy-start.2 = (f32[2,128,128]{2,1,0:T(8,128)S(1)}, f32[2,128,128]{2,1,0:T(8,128)}, u32[]{:S(2)}) copy-start(f32[2,128,128]{2,1,0:T(8,128)} %probe_ref.1) | copy-start | bytes 393220
  1.9 1.0 %copy-start = (bf16[4,256,256]{2,1,0:T(8,128)(2,1)S(1)}, bf16[4,256,256]{2,1,0:T(8,128)(2,1)}, u32[]{:S(2)}) copy-start(bf16[4,256,256]{2,1,0:T(8,128)(2,1)} %constant.4.clone.table_ref) | copy-start | bytes 1572868
  3.0 0.9 %copy-start.3 = (f32[2,128,128]{2,1,0:T(8,128)S(1)}, f32[2,128,128]{2,1,0:T(8,128)}, u32[]{:S(2)}) copy-start(f32[2,128,128]{2,1,0:T(8,128)} %constant.5.clone.mover_ref) | copy-start | bytes 393220

commit v2 on v1

--- a/solution.py
+++ b/solution.py
@@ -27,11 +27,10 @@
     im = -np.sin(angle) / math.sqrt(window)
     forward = np.block([[re, im], [-im, re]])
     high, low = halves(forward)
-    high_t, low_t = halves(forward.T)
     frequency = np.where(index < window // 2, index, index - window) / window
     phase = -60.0 * (frequency[:, None] ** 2 + frequency[None, :] ** 2)
     mover = np.stack([np.cos(phase), np.sin(phase)]).astype(np.float32)
-    return np.stack([high, low, high_t, low_t]), mover
+    return np.stack([high, low]), mover
 
 
 def split(values):
@@ -41,12 +40,14 @@
 
 
 def product(left, right):
-    dot = functools.partial(jnp.dot, preferred_element_type=jnp.float32)
-    return dot(left[0], right[0]) + (dot(left[1], right[0]) + dot(left[0], right[1]))
+    wide = jnp.concatenate([left[0], left[1], left[0]], axis=1)
+    tall = jnp.concatenate([right[0], right[0], right[1]], axis=0)
+    return jnp.dot(wide, tall, preferred_element_type=jnp.float32)
 
 
 def kernel(
-    sizes, pos_ref, obj_ref, probe_ref, intensity_ref, table_ref, mover_ref, out_ref,
+    sizes, pos_ref, obj_ref, probe_hbm, intensity_hbm, table_hbm, mover_hbm, out_ref,
+    probe_ref, intensity_ref, table_ref, mover_ref, load_sem,
     tiles, canvas, spread, give, take, total, final,
     tile_send, tile_recv, sum_send, sum_recv,
 ):
@@ -75,8 +76,22 @@
     ]
     for peer in peers:
         pl.semaphore_signal(barrier, inc=1, device_id=peer, device_id_type=MESH)
+    loads = [
+        pltpu.make_async_copy(source, target, load_sem.at[i])
+        for i, (source, target) in enumerate(
+            [
+                (probe_hbm, probe_ref),
+                (table_hbm, table_ref),
+                (mover_hbm, mover_ref),
+                (intensity_hbm, intensity_ref),
+            ]
+        )
+    ]
+    for load in loads:
+        load.start()
     for layer in range(layers):
-        tiles[layer, 0, 0, 0] = jnp.concatenate([obj_ref[layer, 0], obj_ref[layer, 1]], axis=1)
+        both = jnp.concatenate([obj_ref[layer, 0], obj_ref[layer, 1]], axis=0)
+        tiles[layer, 0, 0, 0] = both.T
     margin = jnp.zeros((window, window), jnp.float32)
     for n in range(items):
         for plane in range(2):
@@ -127,7 +142,7 @@
 
     away = places[1:]
     for layer in range(layers):
-        for b, d in away:
+        for b, d in away[::-1]:
             tile_copy(layer, b, d).start()
         tile_pass(layer, 0, 0).start()
 
@@ -146,8 +161,8 @@
             canvas[layer, 0, d, rows] = jnp.where(in_left, west, pltpu.roll(east, half, 1))
             canvas[layer, 1, d, rows] = jnp.where(in_left, pltpu.roll(west, half, 1), east)
 
-    row = [pos_ref[0, n, 0] for n in range(items)]
-    col = [(pos_ref[0, n, 1] + columns - chip * window) % columns for n in range(items)]
+    row = [pos_ref[0, 0, n] for n in range(items)]
+    col = [(pos_ref[0, 1, n] + columns - chip * window) % columns for n in range(items)]
 
     def cut(layer):
         patches = []
@@ -162,37 +177,36 @@
             patches.append(tuple(both))
         return patches
 
-    def on_rows(waves, which):
+    def on_rows(waves):
         stacked = jnp.concatenate([jnp.concatenate(w, axis=1) for w in waves], axis=0)
-        matrix = (table_ref[2 * which], table_ref[2 * which + 1])
-        out = product(split(stacked), matrix)
+        out = product(split(stacked), (table_ref[0], table_ref[1]))
         return [
             (out[n * window : (n + 1) * window, :window], out[n * window : (n + 1) * window, window:])
             for n in range(len(waves))
         ]
 
-    def on_columns(waves, which):
+    def on_columns(waves):
         stacked = jnp.concatenate([jnp.concatenate(w, axis=0) for w in waves], axis=1)
-        matrix = (table_ref[2 - 2 * which], table_ref[3 - 2 * which])
-        out = product(matrix, split(stacked))
+        out = product((table_ref[0], table_ref[1]), split(stacked))
         return [
             (out[:window, n * window : (n + 1) * window], out[window:, n * window : (n + 1) * window])
             for n in range(len(waves))
         ]
 
+    def swap(waves):
+        return [(w[1], w[0]) for w in waves]
+
     def forward(waves):
-        return on_rows(on_columns(waves, 0), 0)
+        return on_rows(swap(on_columns(swap(waves))))
 
     def backward(waves):
-        return on_columns(on_rows(waves, 1), 1)
+        return on_columns(swap(on_rows(swap(waves))))
 
     def times(a, b):
         return (a[0] * b[0] - a[1] * b[1], a[0] * b[1] + a[1] * b[0])
 
     def conj_times(a, b):
         return (a[0] * b[0] + a[1] * b[1], a[0] * b[1] - a[1] * b[0])
-
-    mover = (mover_ref[0], mover_ref[1])
 
     def scatter(layer, grads):
         blank = jnp.zeros((window, columns - window), jnp.float32)
@@ -202,7 +216,7 @@
                 wide = pltpu.roll(wide, col[n], 1)
                 for d in range(chips):
                     spread[n, plane, d, window : 2 * window] = wide[:, d * window : (d + 1) * window]
-        for b, d in places:
+        for b, d in away[::-1] + places[:1]:
             re, im = [
                 sum(
                     spread[n, plane, d, pl.ds((b + 1) * window - row[n], window), :]
@@ -217,13 +231,16 @@
             sum_pass(layer, b, d).start()
 
     def share(layer):
-        for b, d in away + places[:1]:
+        for b, d in away[::-1] + places[:1]:
             sum_pass(layer, b, d).wait_recv()
             total[layer, b, d] = total[layer, b, d] + take[layer, b, d]
             if (b, d) != (0, 0):
                 sum_copy(layer, b, d).start()
 
     relay(0)
+    for load in loads:
+        load.wait()
+    mover = (mover_ref[0], mover_ref[1])
     assemble(0)
     incident = [[(probe_ref[0], probe_ref[1])] * items]
     patches = []
@@ -255,8 +272,9 @@
             sum_copy(layer, b, d).wait_recv()
             value = value + final[layer, b, d]
         value = value * scale
-        out_ref[layer, 0] = value[:, :half]
-        out_ref[layer, 1] = value[:, half:]
+        value = value.T
+        out_ref[layer, 0] = value[:half]
+        out_ref[layer, 1] = value[half:]
     for layer in range(layers):
         for b, d in places:
             tile_pass(layer, b, d).wait_send()
@@ -275,12 +293,19 @@
     table, mover = tables(window)
     f32 = jnp.float32
     whole = pl.BlockSpec(memory_space=pltpu.VMEM)
-    return pl.pallas_call(
+    kept = pl.BlockSpec(memory_space=pltpu.HBM)
+    turned = object_slices.transpose(0, 1, 3, 2)
+    result = pl.pallas_call(
         functools.partial(kernel, (layers, chips, regions, items, window)),
-        out_shape=jax.ShapeDtypeStruct(object_slices.shape, f32),
-        in_specs=[pl.BlockSpec(memory_space=pltpu.SMEM)] + [whole] * 5,
+        out_shape=jax.ShapeDtypeStruct(turned.shape, f32),
+        in_specs=[pl.BlockSpec(memory_space=pltpu.SMEM), whole] + [kept] * 4,
         out_specs=whole,
         scratch_shapes=[
+            pltpu.VMEM(probe.shape, f32),
+            pltpu.VMEM(intensity.shape, f32),
+            pltpu.VMEM(table.shape, jnp.bfloat16),
+            pltpu.VMEM(mover.shape, f32),
+            pltpu.SemaphoreType.DMA((4,)),
             pltpu.VMEM((layers, 2, chips, 2, window, window), f32),
             pltpu.VMEM((layers, 2, chips, 2 * window, window), f32),
             pltpu.VMEM((items, 2, chips, 3 * window, window), f32),
@@ -293,7 +318,8 @@
         compiler_params=pltpu.CompilerParams(
             collective_id=0, has_side_effects=True, vmem_limit_bytes=VMEM_BYTES
         ),
-    )(positions, object_slices, probe, intensity, jnp.asarray(table), jnp.asarray(mover))
+    )(positions.transpose(0, 2, 1), turned, probe, intensity, jnp.asarray(table), jnp.asarray(mover))
+    return result.transpose(0, 1, 3, 2)
 
 
 def solution(mesh):

time: 34.9 us -> 35.5 us (1.017)
  local copies, waits for them, and re-layouts: 4.6 us -> 5.95 us
  Pallas kernels: 30.1 us -> 29.3 us
    unnamed x10 -> x13, local copies, waits for them, and re-layouts: 3.82 us -> 5.95 us
    pallas_call x1 -> x0, local copies, waits for them, and re-layouts: 0.77 us -> none  [body(): pl.pallas_call(functools.partial(kernel, (layers, chips, regions, items,...]
    pallas_call x1, Pallas kernels: 30.1 us -> 29.3 us  [body(): pl.pallas_call(functools.partial(kernel, (layers, chips, regions, items,...]
where the time goes in v2:
time: 35.5 us; the launch traced here: 35.3 us
  Pallas kernels  29.3 us (83%)
  local copies, waits for them, and re-layouts  5.95 us (17%)
    pallas_call x1, Pallas kernels, body(): pl.pallas_call(functools.partial(kernel, (layers, chips, regions, items,...  29.3 us
    unnamed x13, local copies, waits for them, and re-layouts  5.95 us

profile of v2, /device:TPU:0, one launch (start us, length us, event | category | flops | bytes accessed | tf_op | source)
XLA Modules:
  0.0 35.3 jit_solution(16425165093448146286)
XLA Ops:
  0.0 0.0 copy-start.5
  0.0 0.7 %copy-done.5 = s32[1,4,2]{1,2,0:T(2,128)S(1)} copy-done((s32[1,4,2]{1,2,0:T(2,128)S(1)}, s32[1,4,2]{1,2,0:T(2,128)}, u32[]{:S(2)}) %copy-start.5) | copy-done | bytes 56
  0.7 0.0 copy-start
  0.7 0.9 %copy-done = f32[1,4,128,128]{3,2,1,0:T(8,128)S(1)} copy-done((f32[1,4,128,128]{3,2,1,0:T(8,128)S(1)}, f32[1,4,128,128]{3,2,1,0:T(8,128)}, u32[]{:S(2)}) %copy-start) | copy-done | bytes 262168
  1.6 0.0 copy-start.1
  1.6 0.9 %copy-done.1 = bf16[2,256,256]{2,1,0:T(8,128)(2,1)S(1)} copy-done((bf16[2,256,256]{2,1,0:T(8,128)(2,1)S(1)}, bf16[2,256,256]{2,1,0:T(8,128)(2,1)}, u32[]{:S(2)}) %copy-start.1) | copy-done | bytes 262168
  2.6 0.0 copy-start.2
  2.6 0.9 %copy-done.2 = f32[2,2,128,64]{2,3,1,0:T(8,128)S(1)} copy-done((f32[2,2,128,64]{2,3,1,0:T(8,128)S(1)}, f32[2,2,128,64]{2,3,1,0:T(8,128)}, u32[]{:S(2)}) %copy-start.2) | copy-done | bytes 131096
  3.5 0.0 copy-start.3
  3.5 0.9 %copy-done.3 = f32[2,128,128]{2,1,0:T(8,128)S(1)} copy-done((f32[2,128,128]{2,1,0:T(8,128)S(1)}, f32[2,128,128]{2,1,0:T(8,128)}, u32[]{:S(2)}) %copy-start.3) | copy-done | bytes 131096
  4.4 0.0 copy-start.4
  4.4 0.9 %copy-done.4 = f32[2,128,128]{2,1,0:T(8,128)S(1)} copy-done((f32[2,128,128]{2,1,0:T(8,128)S(1)}, f32[2,128,128]{2,1,0:T(8,128)}, u32[]{:S(2)}) %copy-start.4) | copy-done | bytes 131096
  5.3 29.3 %shard_map.64 = f32[2,2,64,128]{3,2,1,0:T(8,128)S(1)} custom-call(s32[1,2,4]{2,1,0:T(2,128)S(1)} %bitcast.5, f32[2,2,64,128]{3,2,1,0:T(8,128)S(1)} %bitcast.4, f32[2,128,128]{2,1,0:T(8,128)S(1)} %copy-done.3, f32[1,4,128,128]{3,2,1,0:T(8,128)S(1)} %copy-done, bf16[2,256,256]{2,1,0:T(8,128)(2,1)S(1)} %copy-done.1, f32[2,128,128]{2,1,0:T(8,128)S(1)} %copy-done.4), custom_call_target="tpu_custom_call" | custom-call | tf_op jit(solution)/shard_map/pallas_call | solution.py:298
  34.6 0.7 %copy.8 = f32[2,2,128,64]{2,3,1,0:T(8,128)} copy(f32[2,2,128,64]{2,3,1,0:T(8,128)S(1)} %bitcast.3) | data formatting | bytes 262144
Async XLA Ops:
  0.0 0.7 %copy-start.5 = (s32[1,4,2]{1,2,0:T(2,128)S(1)}, s32[1,4,2]{1,2,0:T(2,128)}, u32[]{:S(2)}) copy-start(s32[1,4,2]{1,2,0:T(2,128)} %param.9) | copy-start | bytes 100
  0.7 0.9 %copy-start = (f32[1,4,128,128]{3,2,1,0:T(8,128)S(1)}, f32[1,4,128,128]{3,2,1,0:T(8,128)}, u32[]{:S(2)}) copy-start(f32[1,4,128,128]{3,2,1,0:T(8,128)} %intensity_hbm.1) | copy-start | bytes 786436
  1.6 0.9 %copy-start.1 = (bf16[2,256,256]{2,1,0:T(8,128)(2,1)S(1)}, bf16[2,256,256]{2,1,0:T(8,128)(2,1)}, u32[]{:S(2)}) copy-start(bf16[2,256,256]{2,1,0:T(8,128)(2,1)} %constant.4.clone.table_hbm) | copy-start | bytes 786436
  2.6 0.9 %copy-start.2 = (f32[2,2,128,64]{2,3,1,0:T(8,128)S(1)}, f32[2,2,128,64]{2,3,1,0:T(8,128)}, u32[]{:S(2)}) copy-start(f32[2,2,128,64]{2,3,1,0:T(8,128)} %param.6) | copy-start | bytes 393220
  3.5 0.9 %copy-start.3 = (f32[2,128,128]{2,1,0:T(8,128)S(1)}, f32[2,128,128]{2,1,0:T(8,128)}, u32[]{:S(2)}) copy-start(f32[2,128,128]{2,1,0:T(8,128)} %probe_hbm.1) | copy-start | bytes 393220
  4.4 0.9 %copy-start.4 = (f32[2,128,128]{2,1,0:T(8,128)S(1)}, f32[2,128,128]{2,1,0:T(8,128)}, u32[]{:S(2)}) copy-start(f32[2,128,128]{2,1,0:T(8,128)} %constant.5.clone.mover_hbm) | copy-start | bytes 393220

commit v3 on v2

--- a/solution.py
+++ b/solution.py
@@ -293,7 +293,7 @@
     table, mover = tables(window)
     f32 = jnp.float32
     whole = pl.BlockSpec(memory_space=pltpu.VMEM)
-    kept = pl.BlockSpec(memory_space=pltpu.HBM)
+    kept = pl.BlockSpec(memory_space=pl.ANY)
     turned = object_slices.transpose(0, 1, 3, 2)
     result = pl.pallas_call(
         functools.partial(kernel, (layers, chips, regions, items, window)),

time: 35.5 us -> 35.5 us (level)
  no operation moved by 1% of the time
where the time goes in v3:
time: 35.5 us; the launch traced here: 35.2 us
  Pallas kernels  29.3 us (83%)
  local copies, waits for them, and re-layouts  5.95 us (17%)
    pallas_call x1, Pallas kernels, body(): pl.pallas_call(functools.partial(kernel, (layers, chips, regions, items,...  29.3 us
    unnamed x13, local copies, waits for them, and re-layouts  5.95 us

profile of v3, /device:TPU:0, one launch (start us, length us, event | category | flops | bytes accessed | tf_op | source)
XLA Modules:
  0.0 35.2 jit_solution(16425165093448146286)
XLA Ops:
  0.0 0.0 copy-start.5
  0.0 0.7 %copy-done.5 = s32[1,4,2]{1,2,0:T(2,128)S(1)} copy-done((s32[1,4,2]{1,2,0:T(2,128)S(1)}, s32[1,4,2]{1,2,0:T(2,128)}, u32[]{:S(2)}) %copy-start.5) | copy-done | bytes 56
  0.7 0.0 copy-start
  0.7 0.9 %copy-done = f32[1,4,128,128]{3,2,1,0:T(8,128)S(1)} copy-done((f32[1,4,128,128]{3,2,1,0:T(8,128)S(1)}, f32[1,4,128,128]{3,2,1,0:T(8,128)}, u32[]{:S(2)}) %copy-start) | copy-done | bytes 262168
  1.6 0.0 copy-start.1
  1.6 0.9 %copy-done.1 = bf16[2,256,256]{2,1,0:T(8,128)(2,1)S(1)} copy-done((bf16[2,256,256]{2,1,0:T(8,128)(2,1)S(1)}, bf16[2,256,256]{2,1,0:T(8,128)(2,1)}, u32[]{:S(2)}) %copy-start.1) | copy-done | bytes 262168
  2.6 0.0 copy-start.2
  2.6 0.9 %copy-done.2 = f32[2,2,128,64]{2,3,1,0:T(8,128)S(1)} copy-done((f32[2,2,128,64]{2,3,1,0:T(8,128)S(1)}, f32[2,2,128,64]{2,3,1,0:T(8,128)}, u32[]{:S(2)}) %copy-start.2) | copy-done | bytes 131096
  3.5 0.0 copy-start.3
  3.5 0.9 %copy-done.3 = f32[2,128,128]{2,1,0:T(8,128)S(1)} copy-done((f32[2,128,128]{2,1,0:T(8,128)S(1)}, f32[2,128,128]{2,1,0:T(8,128)}, u32[]{:S(2)}) %copy-start.3) | copy-done | bytes 131096
  4.4 0.0 copy-start.4
  4.4 0.9 %copy-done.4 = f32[2,128,128]{2,1,0:T(8,128)S(1)} copy-done((f32[2,128,128]{2,1,0:T(8,128)S(1)}, f32[2,128,128]{2,1,0:T(8,128)}, u32[]{:S(2)}) %copy-start.4) | copy-done | bytes 131096
  5.3 29.3 %shard_map.64 = f32[2,2,64,128]{3,2,1,0:T(8,128)S(1)} custom-call(s32[1,2,4]{2,1,0:T(2,128)S(1)} %bitcast.5, f32[2,2,64,128]{3,2,1,0:T(8,128)S(1)} %bitcast.4, f32[2,128,128]{2,1,0:T(8,128)S(1)} %copy-done.3, f32[1,4,128,128]{3,2,1,0:T(8,128)S(1)} %copy-done, bf16[2,256,256]{2,1,0:T(8,128)(2,1)S(1)} %copy-done.1, f32[2,128,128]{2,1,0:T(8,128)S(1)} %copy-done.4), custom_call_target="tpu_custom_call" | custom-call | tf_op jit(solution)/shard_map/pallas_call | solution.py:298
  34.6 0.7 %copy.8 = f32[2,2,128,64]{2,3,1,0:T(8,128)} copy(f32[2,2,128,64]{2,3,1,0:T(8,128)S(1)} %bitcast.3) | data formatting | bytes 262144
Async XLA Ops:
  0.0 0.7 %copy-start.5 = (s32[1,4,2]{1,2,0:T(2,128)S(1)}, s32[1,4,2]{1,2,0:T(2,128)}, u32[]{:S(2)}) copy-start(s32[1,4,2]{1,2,0:T(2,128)} %param.9) | copy-start | bytes 100
  0.7 0.9 %copy-start = (f32[1,4,128,128]{3,2,1,0:T(8,128)S(1)}, f32[1,4,128,128]{3,2,1,0:T(8,128)}, u32[]{:S(2)}) copy-start(f32[1,4,128,128]{3,2,1,0:T(8,128)} %intensity_hbm.1) | copy-start | bytes 786436
  1.6 0.9 %copy-start.1 = (bf16[2,256,256]{2,1,0:T(8,128)(2,1)S(1)}, bf16[2,256,256]{2,1,0:T(8,128)(2,1)}, u32[]{:S(2)}) copy-start(bf16[2,256,256]{2,1,0:T(8,128)(2,1)} %constant.4.clone.table_hbm) | copy-start | bytes 786436
  2.6 0.9 %copy-start.2 = (f32[2,2,128,64]{2,3,1,0:T(8,128)S(1)}, f32[2,2,128,64]{2,3,1,0:T(8,128)}, u32[]{:S(2)}) copy-start(f32[2,2,128,64]{2,3,1,0:T(8,128)} %param.6) | copy-start | bytes 393220
  3.5 0.9 %copy-start.3 = (f32[2,128,128]{2,1,0:T(8,128)S(1)}, f32[2,128,128]{2,1,0:T(8,128)}, u32[]{:S(2)}) copy-start(f32[2,128,128]{2,1,0:T(8,128)} %probe_hbm.1) | copy-start | bytes 393220
  4.4 0.9 %copy-start.4 = (f32[2,128,128]{2,1,0:T(8,128)S(1)}, f32[2,128,128]{2,1,0:T(8,128)}, u32[]{:S(2)}) copy-start(f32[2,128,128]{2,1,0:T(8,128)} %constant.5.clone.mover_hbm) | copy-start | bytes 393220

commit v4 on v1

--- a/solution.py
+++ b/solution.py
@@ -23,15 +23,13 @@
 def tables(window):
     index = np.arange(window)
     angle = (index[:, None] * index[None, :] % window) * (2.0 * math.pi / window)
-    re = np.cos(angle) / math.sqrt(window)
-    im = -np.sin(angle) / math.sqrt(window)
-    forward = np.block([[re, im], [-im, re]])
-    high, low = halves(forward)
-    high_t, low_t = halves(forward.T)
+    dft = np.exp(-1j * angle) / math.sqrt(window)
     frequency = np.where(index < window // 2, index, index - window) / window
-    phase = -60.0 * (frequency[:, None] ** 2 + frequency[None, :] ** 2)
-    mover = np.stack([np.cos(phase), np.sin(phase)]).astype(np.float32)
-    return np.stack([high, low, high_t, low_t]), mover
+    move = dft.conj() @ (np.exp(-60j * frequency**2)[:, None] * dft)
+    parts = []
+    for matrix in (dft, move):
+        parts += halves(np.block([[matrix.real, matrix.imag], [-matrix.imag, matrix.real]]))
+    return np.stack(parts)
 
 
 def split(values):
@@ -41,12 +39,13 @@
 
 
 def product(left, right):
-    dot = functools.partial(jnp.dot, preferred_element_type=jnp.float32)
-    return dot(left[0], right[0]) + (dot(left[1], right[0]) + dot(left[0], right[1]))
+    wide = jnp.concatenate([left[0], left[1], left[0]], axis=1)
+    tall = jnp.concatenate([right[0], right[0], right[1]], axis=0)
+    return jnp.dot(wide, tall, preferred_element_type=jnp.float32)
 
 
 def kernel(
-    sizes, pos_ref, obj_ref, probe_ref, intensity_ref, table_ref, mover_ref, out_ref,
+    sizes, pos_ref, obj_ref, probe_ref, intensity_ref, table_ref, out_ref,
     tiles, canvas, spread, give, take, total, final,
     tile_send, tile_recv, sum_send, sum_recv,
 ):
@@ -173,26 +172,34 @@
 
     def on_columns(waves, which):
         stacked = jnp.concatenate([jnp.concatenate(w, axis=0) for w in waves], axis=1)
-        matrix = (table_ref[2 - 2 * which], table_ref[3 - 2 * which])
+        matrix = (table_ref[2 * which], table_ref[2 * which + 1])
         out = product(matrix, split(stacked))
         return [
             (out[:window, n * window : (n + 1) * window], out[window:, n * window : (n + 1) * window])
             for n in range(len(waves))
         ]
 
-    def forward(waves):
-        return on_rows(on_columns(waves, 0), 0)
-
-    def backward(waves):
-        return on_columns(on_rows(waves, 1), 1)
+    def swap(waves):
+        return [(w[1], w[0]) for w in waves]
+
+    def nothing():
+        pass
+
+    def forward(waves, which, between=nothing):
+        waves = swap(on_columns(swap(waves), which))
+        between()
+        return on_rows(waves, which)
+
+    def backward(waves, which, between=nothing):
+        waves = swap(on_rows(swap(waves), which))
+        between()
+        return on_columns(waves, which)
 
     def times(a, b):
         return (a[0] * b[0] - a[1] * b[1], a[0] * b[1] + a[1] * b[0])
 
     def conj_times(a, b):
         return (a[0] * b[0] + a[1] * b[1], a[0] * b[1] - a[1] * b[0])
-
-    mover = (mover_ref[0], mover_ref[1])
 
     def scatter(layer, grads):
         blank = jnp.zeros((window, columns - window), jnp.float32)
@@ -202,7 +209,7 @@
                 wide = pltpu.roll(wide, col[n], 1)
                 for d in range(chips):
                     spread[n, plane, d, window : 2 * window] = wide[:, d * window : (d + 1) * window]
-        for b, d in places:
+        for b, d in away[::-1] + places[:1]:
             re, im = [
                 sum(
                     spread[n, plane, d, pl.ds((b + 1) * window - row[n], window), :]
@@ -217,7 +224,7 @@
             sum_pass(layer, b, d).start()
 
     def share(layer):
-        for b, d in away + places[:1]:
+        for b, d in away[::-1] + places[:1]:
             sum_pass(layer, b, d).wait_recv()
             total[layer, b, d] = total[layer, b, d] + take[layer, b, d]
             if (b, d) != (0, 0):
@@ -230,23 +237,21 @@
     for layer in range(layers):
         patches.append(cut(layer))
         leaving = [times(w, p) for w, p in zip(incident[layer], patches[layer])]
-        far = forward(leaving)
         if layer < layers - 1:
-            relay(layer + 1)
-            incident.append(backward([times(mover, w) for w in far]))
+            incident.append(forward(leaving, 1, functools.partial(relay, layer + 1)))
             assemble(layer + 1)
+    far = forward(leaving, 0)
     residual = []
     for n in range(items):
         re, im = far[n]
         misfit = re * re + im * im - intensity_ref[0, n]
         residual.append((misfit * re, misfit * im))
-    back = backward(residual)
+    back = backward(residual, 0)
     for layer in reversed(range(layers)):
         scatter(layer, [conj_times(w, g) for w, g in zip(incident[layer], back)])
         if layer > 0:
-            far = forward([conj_times(p, g) for p, g in zip(patches[layer], back)])
-            share(layer)
-            back = backward([conj_times(mover, w) for w in far])
+            carried = [conj_times(p, g) for p, g in zip(patches[layer], back)]
+            back = backward(carried, 1, functools.partial(share, layer))
     share(0)
     scale = 1.0 / (items * 2 * chips)
     for layer in reversed(range(layers)):
@@ -272,13 +277,13 @@
     items = positions.shape[1]
     chips = lax.axis_size("probe") // 2
     regions = lax.axis_size("region")
-    table, mover = tables(window)
+    table = tables(window)
     f32 = jnp.float32
     whole = pl.BlockSpec(memory_space=pltpu.VMEM)
     return pl.pallas_call(
         functools.partial(kernel, (layers, chips, regions, items, window)),
         out_shape=jax.ShapeDtypeStruct(object_slices.shape, f32),
-        in_specs=[pl.BlockSpec(memory_space=pltpu.SMEM)] + [whole] * 5,
+        in_specs=[pl.BlockSpec(memory_space=pltpu.SMEM)] + [whole] * 4,
         out_specs=whole,
         scratch_shapes=[
             pltpu.VMEM((layers, 2, chips, 2, window, window), f32),
@@ -293,7 +298,7 @@
         compiler_params=pltpu.CompilerParams(
             collective_id=0, has_side_effects=True, vmem_limit_bytes=VMEM_BYTES
         ),
-    )(positions, object_slices, probe, intensity, jnp.asarray(table), jnp.asarray(mover))
+    )(positions, object_slices, probe, intensity, jnp.asarray(table))
 
 
 def solution(mesh):

time: 34.9 us -> 32.5 us (0.931)
  Pallas kernels: 30.1 us -> 28.6 us
  local copies, waits for them, and re-layouts: 4.6 us -> 3.69 us
    pallas_call x1, Pallas kernels: 30.1 us -> 28.6 us  [body(): pl.pallas_call(functools.partial(kernel, (layers, chips, regions, items,...]
    unnamed x10 -> x8, local copies, waits for them, and re-layouts: 3.82 us -> 2.92 us
where the time goes in v4:
time: 32.5 us; the launch traced here: 32.3 us
  Pallas kernels  28.6 us (88%)
  local copies, waits for them, and re-layouts  3.69 us (11%)
    pallas_call x1, Pallas kernels, body(): pl.pallas_call(functools.partial(kernel, (layers, chips, regions, items,...  28.6 us
    unnamed x8, local copies, waits for them, and re-layouts  2.92 us
    pallas_call x1, local copies, waits for them, and re-layouts, body(): pl.pallas_call(functools.partial(kernel, (layers, chips, regions, items,...  0.77 us

profile of v4, /device:TPU:0, one launch (start us, length us, event | category | flops | bytes accessed | tf_op | source)
XLA Modules:
  0.0 32.3 jit_solution(2336309645835456045)
XLA Ops:
  0.0 0.0 copy-start.1
  0.0 0.8 %copy.6.pos_ref = s32[1,4,2]{2,1,0:T(4,128)S(1)} copy(s32[1,4,2]{1,2,0:T(2,128)} %param.8) | data formatting | bytes 64 | tf_op args[3]
  0.8 0.0 copy-start.2
  0.8 1.1 %copy.7.obj_ref = f32[2,2,128,64]{3,2,1,0:T(8,128)S(1)} copy(f32[2,2,128,64]{2,3,1,0:T(8,128)} %param.5) | data formatting | bytes 262144 | tf_op args[0]
  1.9 0.0 copy-done.1
  1.9 0.0 copy-done.2
  1.9 0.0 copy-start
  1.9 1.0 %copy-done = bf16[4,256,256]{2,1,0:T(8,128)(2,1)S(1)} copy-done((bf16[4,256,256]{2,1,0:T(8,128)(2,1)S(1)}, bf16[4,256,256]{2,1,0:T(8,128)(2,1)}, u32[]{:S(2)}) %copy-start) | copy-done | bytes 524312
  3.0 28.6 %shard_map.55 = f32[2,2,128,64]{3,2,1,0:T(8,128)S(1)} custom-call(s32[1,4,2]{2,1,0:T(4,128)S(1)} %copy.6.pos_ref, f32[2,2,128,64]{3,2,1,0:T(8,128)S(1)} %copy.7.obj_ref, f32[2,128,128]{2,1,0:T(8,128)S(1)} %copy-done.2, f32[1,4,128,128]{3,2,1,0:T(8,128)S(1)} %copy-done.1, bf16[4,256,256]{2,1,0:T(8,128)(2,1)S(1)} %copy-done), custom_call_target="tpu_custom_call" | custom-call | tf_op jit(solution)/shard_map/pallas_call | solution.py:283
  31.6 0.8 %copy.8 = f32[2,2,128,64]{2,3,1,0:T(8,128)} copy(f32[2,2,128,64]{3,2,1,0:T(8,128)S(1)} %shard_map.55) | data formatting | bytes 262144 | tf_op jit(solution)/shard_map/pallas_call | solution.py:283
Async XLA Ops:
  0.0 1.9 %copy-start.1 = (f32[1,4,128,128]{3,2,1,0:T(8,128)S(1)}, f32[1,4,128,128]{3,2,1,0:T(8,128)}, u32[]{:S(2)}) copy-start(f32[1,4,128,128]{3,2,1,0:T(8,128)} %intensity_ref.1) | copy-start | bytes 786436
  0.8 1.1 %copy-start.2 = (f32[2,128,128]{2,1,0:T(8,128)S(1)}, f32[2,128,128]{2,1,0:T(8,128)}, u32[]{:S(2)}) copy-start(f32[2,128,128]{2,1,0:T(8,128)} %probe_ref.1) | copy-start | bytes 393220
  1.9 1.0 %copy-start = (bf16[4,256,256]{2,1,0:T(8,128)(2,1)S(1)}, bf16[4,256,256]{2,1,0:T(8,128)(2,1)}, u32[]{:S(2)}) copy-start(bf16[4,256,256]{2,1,0:T(8,128)(2,1)} %constant.2.clone.table_ref) | copy-start | bytes 1572868

commit v5 on v4

--- a/solution.py
+++ b/solution.py
@@ -125,8 +125,9 @@
         )
 
     away = places[1:]
-    for layer in range(layers):
-        for b, d in away:
+
+    def launch(layer):
+        for b, d in away[::-1]:
             tile_copy(layer, b, d).start()
         tile_pass(layer, 0, 0).start()
 
@@ -134,6 +135,8 @@
         for b, d in away:
             tile_copy(layer, b, d).wait_recv()
             tile_pass(layer, b, d).start()
+        if layer < layers - 1:
+            launch(layer + 1)
 
     def assemble(layer):
         for b, d in places:
@@ -230,6 +233,7 @@
             if (b, d) != (0, 0):
                 sum_copy(layer, b, d).start()
 
+    launch(0)
     relay(0)
     assemble(0)
     incident = [[(probe_ref[0], probe_ref[1])] * items]

time: 32.5 us -> 33.2 us (1.022)
  Pallas kernels: 28.6 us -> 29.3 us
    pallas_call x1, Pallas kernels: 28.6 us -> 29.3 us  [body(): pl.pallas_call(functools.partial(kernel, (layers, chips, regions, items,...]
where the time goes in v5:
time: 33.2 us; the launch traced here: 33.1 us
  Pallas kernels  29.3 us (88%)
  local copies, waits for them, and re-layouts  3.69 us (11%)
    pallas_call x1, Pallas kernels, body(): pl.pallas_call(functools.partial(kernel, (layers, chips, regions, items,...  29.3 us
    unnamed x8, local copies, waits for them, and re-layouts  2.92 us
    pallas_call x1, local copies, waits for them, and re-layouts, body(): pl.pallas_call(functools.partial(kernel, (layers, chips, regions, items,...  0.77 us

profile of v5, /device:TPU:0, one launch (start us, length us, event | category | flops | bytes accessed | tf_op | source)
XLA Modules:
  0.0 33.1 jit_solution(522168522713148137)
XLA Ops:
  0.0 0.0 copy-start.1
  0.0 0.8 %copy.6.pos_ref = s32[1,4,2]{2,1,0:T(4,128)S(1)} copy(s32[1,4,2]{1,2,0:T(2,128)} %param.8) | data formatting | bytes 64 | tf_op args[3]
  0.8 0.0 copy-start.2
  0.8 1.1 %copy.7.obj_ref = f32[2,2,128,64]{3,2,1,0:T(8,128)S(1)} copy(f32[2,2,128,64]{2,3,1,0:T(8,128)} %param.5) | data formatting | bytes 262144 | tf_op args[0]
  1.9 0.0 copy-done.1
  1.9 0.0 copy-done.2
  1.9 0.0 copy-start
  1.9 1.0 %copy-done = bf16[4,256,256]{2,1,0:T(8,128)(2,1)S(1)} copy-done((bf16[4,256,256]{2,1,0:T(8,128)(2,1)S(1)}, bf16[4,256,256]{2,1,0:T(8,128)(2,1)}, u32[]{:S(2)}) %copy-start) | copy-done | bytes 524312
  3.0 29.3 %shard_map.55 = f32[2,2,128,64]{3,2,1,0:T(8,128)S(1)} custom-call(s32[1,4,2]{2,1,0:T(4,128)S(1)} %copy.6.pos_ref, f32[2,2,128,64]{3,2,1,0:T(8,128)S(1)} %copy.7.obj_ref, f32[2,128,128]{2,1,0:T(8,128)S(1)} %copy-done.2, f32[1,4,128,128]{3,2,1,0:T(8,128)S(1)} %copy-done.1, bf16[4,256,256]{2,1,0:T(8,128)(2,1)S(1)} %copy-done), custom_call_target="tpu_custom_call" | custom-call | tf_op jit(solution)/shard_map/pallas_call | solution.py:287
  32.3 0.8 %copy.8 = f32[2,2,128,64]{2,3,1,0:T(8,128)} copy(f32[2,2,128,64]{3,2,1,0:T(8,128)S(1)} %shard_map.55) | data formatting | bytes 262144 | tf_op jit(solution)/shard_map/pallas_call | solution.py:287
Async XLA Ops:
  0.0 1.9 %copy-start.1 = (f32[1,4,128,128]{3,2,1,0:T(8,128)S(1)}, f32[1,4,128,128]{3,2,1,0:T(8,128)}, u32[]{:S(2)}) copy-start(f32[1,4,128,128]{3,2,1,0:T(8,128)} %intensity_ref.1) | copy-start | bytes 786436
  0.8 1.1 %copy-start.2 = (f32[2,128,128]{2,1,0:T(8,128)S(1)}, f32[2,128,128]{2,1,0:T(8,128)}, u32[]{:S(2)}) copy-start(f32[2,128,128]{2,1,0:T(8,128)} %probe_ref.1) | copy-start | bytes 393220
  1.9 1.0 %copy-start = (bf16[4,256,256]{2,1,0:T(8,128)(2,1)S(1)}, bf16[4,256,256]{2,1,0:T(8,128)(2,1)}, u32[]{:S(2)}) copy-start(bf16[4,256,256]{2,1,0:T(8,128)(2,1)} %constant.2.clone.table_ref) | copy-start | bytes 1572868

commit v6 on v4

--- a/solution.py
+++ b/solution.py
@@ -162,6 +162,8 @@
         return patches
 
     def on_rows(waves, which):
+        if len(waves) > 2:
+            return on_rows(waves[:2], which) + on_rows(waves[2:], which)
         stacked = jnp.concatenate([jnp.concatenate(w, axis=1) for w in waves], axis=0)
         matrix = (table_ref[2 * which], table_ref[2 * which + 1])
         out = product(split(stacked), matrix)
@@ -171,6 +173,8 @@
         ]
 
     def on_columns(waves, which):
+        if len(waves) > 2:
+            return on_columns(waves[:2], which) + on_columns(waves[2:], which)
         stacked = jnp.concatenate([jnp.concatenate(w, axis=0) for w in waves], axis=1)
         matrix = (table_ref[2 * which], table_ref[2 * which + 1])
         out = product(matrix, split(stacked))

time: 32.5 us -> 32.3 us (level)
  no operation moved by 1% of the time
where the time goes in v6:
time: 32.3 us; the launch traced here: 32.1 us
  Pallas kernels  28.4 us (88%)
  local copies, waits for them, and re-layouts  3.69 us (11%)
    pallas_call x1, Pallas kernels, body(): pl.pallas_call(functools.partial(kernel, (layers, chips, regions, items,...  28.4 us
    unnamed x8, local copies, waits for them, and re-layouts  2.92 us
    pallas_call x1, local copies, waits for them, and re-layouts, body(): pl.pallas_call(functools.partial(kernel, (layers, chips, regions, items,...  0.77 us

profile of v6, /device:TPU:0, one launch (start us, length us, event | category | flops | bytes accessed | tf_op | source)
XLA Modules:
  0.0 32.1 jit_solution(10903213664178705257)
XLA Ops:
  0.0 0.0 copy-start.1
  0.0 0.8 %copy.6.pos_ref = s32[1,4,2]{2,1,0:T(4,128)S(1)} copy(s32[1,4,2]{1,2,0:T(2,128)} %param.8) | data formatting | bytes 64 | tf_op args[3]
  0.8 0.0 copy-start.2
  0.8 1.1 %copy.7.obj_ref = f32[2,2,128,64]{3,2,1,0:T(8,128)S(1)} copy(f32[2,2,128,64]{2,3,1,0:T(8,128)} %param.5) | data formatting | bytes 262144 | tf_op args[0]
  1.9 0.0 copy-done.1
  1.9 0.0 copy-done.2
  1.9 0.0 copy-start
  1.9 1.0 %copy-done = bf16[4,256,256]{2,1,0:T(8,128)(2,1)S(1)} copy-done((bf16[4,256,256]{2,1,0:T(8,128)(2,1)S(1)}, bf16[4,256,256]{2,1,0:T(8,128)(2,1)}, u32[]{:S(2)}) %copy-start) | copy-done | bytes 524312
  3.0 28.4 %shard_map.55 = f32[2,2,128,64]{3,2,1,0:T(8,128)S(1)} custom-call(s32[1,4,2]{2,1,0:T(4,128)S(1)} %copy.6.pos_ref, f32[2,2,128,64]{3,2,1,0:T(8,128)S(1)} %copy.7.obj_ref, f32[2,128,128]{2,1,0:T(8,128)S(1)} %copy-done.2, f32[1,4,128,128]{3,2,1,0:T(8,128)S(1)} %copy-done.1, bf16[4,256,256]{2,1,0:T(8,128)(2,1)S(1)} %copy-done), custom_call_target="tpu_custom_call" | custom-call | tf_op jit(solution)/shard_map/pallas_call | solution.py:287
  31.4 0.8 %copy.8 = f32[2,2,128,64]{2,3,1,0:T(8,128)} copy(f32[2,2,128,64]{3,2,1,0:T(8,128)S(1)} %shard_map.55) | data formatting | bytes 262144 | tf_op jit(solution)/shard_map/pallas_call | solution.py:287
Async XLA Ops:
  0.0 1.9 %copy-start.1 = (f32[1,4,128,128]{3,2,1,0:T(8,128)S(1)}, f32[1,4,128,128]{3,2,1,0:T(8,128)}, u32[]{:S(2)}) copy-start(f32[1,4,128,128]{3,2,1,0:T(8,128)} %intensity_ref.1) | copy-start | bytes 786436
  0.8 1.1 %copy-start.2 = (f32[2,128,128]{2,1,0:T(8,128)S(1)}, f32[2,128,128]{2,1,0:T(8,128)}, u32[]{:S(2)}) copy-start(f32[2,128,128]{2,1,0:T(8,128)} %probe_ref.1) | copy-start | bytes 393220
  1.9 1.0 %copy-start = (bf16[4,256,256]{2,1,0:T(8,128)(2,1)S(1)}, bf16[4,256,256]{2,1,0:T(8,128)(2,1)}, u32[]{:S(2)}) copy-start(bf16[4,256,256]{2,1,0:T(8,128)(2,1)} %constant.2.clone.table_ref) | copy-start | bytes 1572868
